TPU v7x, 32 devices: a whole 2x2x4 slice. The times are simulated.
32 devices in a mesh: dp: 16 (over z, y, x), mp: 2 (over core).
Axes of the slice: x: 2, y: 2, z: 4, core: 2. Of those that a mesh axis runs over, the one named last changes fastest.
Arguments:
- tokens: bfloat16 [25216, 384], P('dp'), may hold values from -6 to 6
- cotangent: bfloat16 [25216, 384], P('dp'), may hold values from -6 to 6
- queue: bfloat16 [2048, 384], P('dp'), may hold values from -6 to 6
- nbr_index: int32 [128, 8], P('dp'), may hold values from 0 to 2047
- nbr_valid: int32 [128, 8], P('dp'), may hold values 0 or 1
- norm_params: float32 [4, 384], replicated, may hold values from -1 to 2.41, as said below
- norm_first: float32 [4, 384], replicated, may hold values from -160 to 160
- norm_second: float32 [4, 384], replicated, may hold values from 2773.76 to 11347.2
- attn_weight: float32 [4, 384, 384], P(None, None, 'mp'), may hold values from -0.8164966 to 0.8164966
- mlp_weight: float32 [2, 384, 1536], P(None, None, 'mp'), may hold values from -0.21875 to 0.21875
- attn_first: float32 [4, 384, 384], P(None, None, 'mp'), may hold values from -104.80501 to 104.80501
- attn_second: float32 [4, 384, 384], P(None, None, 'mp'), may hold values from 118.5152 to 11952.384
- mlp_first: float32 [2, 384, 1536], P(None, None, 'mp'), may hold values from -48 to 48
- mlp_second: float32 [2, 384, 1536], P(None, None, 'mp'), may hold values from 264.768 to 1059.072
- attn_left: float32 [4, 768, 384], P(None, 'mp'), may hold values from -0.03827328 to 1.0382733, as said below
- attn_right: float32 [4, 384, 192], P(None, 'mp'), may hold values from -0.054126588 to 1.0541266, as said below
- mlp_left: float32 [2, 768, 384], P(None, 'mp'), may hold values from -0.03827328 to 1.0382733, as said below
- mlp_right: float32 [2, 1536, 768], P(None, 'mp'), may hold values from -0.027063294 to 1.0270633, as said below
Outputs:
- block_out: bfloat16 [25216, 384], P('dp')
- input_grad: float32 [25216, 384], P('dp')
- norm_grad: float32 [4, 384], replicated
- attn_grad: float32 [4, 384, 384], P(None, None, 'mp')
- mlp_grad: float32 [2, 384, 1536], P(None, None, 'mp')
- norm_first_new: float32 [4, 384], replicated
- norm_second_new: float32 [4, 384], replicated
- norm_new: float32 [4, 384], replicated
- attn_first_new: float32 [4, 384, 384], P(None, None, 'mp')
- attn_second_new: float32 [4, 384, 384], P(None, None, 'mp')
- mlp_first_new: float32 [2, 384, 1536], P(None, None, 'mp')
- mlp_second_new: float32 [2, 384, 1536], P(None, None, 'mp')
- attn_left_new: float32 [4, 768, 384], P(None, 'mp')
- attn_right_new: float32 [4, 384, 192], P(None, 'mp')
- mlp_left_new: float32 [2, 768, 384], P(None, 'mp')
- mlp_right_new: float32 [2, 1536, 768], P(None, 'mp')
- attn_new: float32 [4, 384, 384], P(None, None, 'mp')
- attn_copy: bfloat16 [4, 384, 384], P(None, None, 'mp')
- mlp_new: float32 [2, 384, 1536], P(None, None, 'mp')
- mlp_copy: bfloat16 [2, 384, 1536], P(None, None, 'mp')
Inputs may be any that keep to these rules, and one draw needn't show every extreme that they name: `norm_params`: rows 0 and 2 are positive gains, rows 1 and 3 shifts. `attn_left`: each block of rows is a full-rank basis. `attn_right`: each block of rows is a full-rank basis. `mlp_left`: each block of rows is a full-rank basis. `mlp_right`: each block of rows is a full-rank basis.
All inputs are finite; a program needn't handle non-finite values. No bound on the sum of `nbr_valid` on one device may be relied on, other than what follows from the above.
Results may differ from a plain program's by a relative error of at most 0.0095.
The roundings to bfloat16 on the way count: a program that leaves them out, or rounds other values in their place, can miss the bound.
Values may be sent and summed in bfloat16 or wider, within the bound.
A program may use at most 256 MiB of HBM per device.

v0:
```python
import jax
import jax.numpy as jnp
from jax import lax
from jax.sharding import PartitionSpec as P

P_SIZE = 197
NBR = 8
STEP = 10
HEAD = 64


BETA_FIRST = 0.9
BETA_SECOND = 0.95
EPSILON = 1e-08
RATE_MATRIX = 0.15
RATE_NORM = 0.6
DECAY_RATE = 0.05
TURN_RATE = 4.0


def mult(left, right):
    return jnp.dot(left, right, preferred_element_type=jnp.float32)


def mult_right_t(left, right):
    return lax.dot_general(
        left, right, (((1,), (1,)), ((), ())), preferred_element_type=jnp.float32
    )


def mult_left_t(left, right):
    return lax.dot_general(
        left, right, (((0,), (0,)), ((), ())), preferred_element_type=jnp.float32
    )


def product(left, right):
    return jnp.dot(left, right, precision=lax.Precision.HIGHEST)


def layer_norm(values, gain, shift):
    centre = values - jnp.mean(values, axis=-1, keepdims=True)
    scale = lax.rsqrt(jnp.mean(centre * centre, axis=-1, keepdims=True) + 1e-06)
    normal = centre * scale
    return (normal * gain + shift, normal, scale)


def norm_back(grad, normal, scale, gain):
    shaped = grad * gain
    return scale * (
        shaped
        - jnp.mean(shaped, axis=-1, keepdims=True)
        - normal * jnp.mean(shaped * normal, axis=-1, keepdims=True)
    )


def fetch_rows(queue, nbr_index):
    wanted = nbr_index.reshape(-1)
    piece = lax.all_gather(queue, "dp", axis=0, tiled=True)
    places = lax.iota(jnp.int32, piece.shape[0])
    chooser = (wanted[:, None] == places[None, :]).astype(jnp.bfloat16)
    return mult(chooser, piece).astype(jnp.bfloat16)


def forward(tokens, norms, attn_low, mlp_low, neighbours, nbr_valid):
    images = nbr_valid.shape[0]
    width = attn_low.shape[2]
    heads = width // HEAD
    own_shape = (images, P_SIZE, heads, HEAD)
    far_shape = (images, NBR, heads, HEAD)
    normed_f, normal_one, scale_one = layer_norm(tokens, norms[0], norms[1])
    normed = normed_f.astype(jnp.bfloat16)
    quest = mult(normed, attn_low[0]).astype(jnp.bfloat16).reshape(own_shape)
    keys = jnp.concatenate(
        [
            mult(normed, attn_low[1]).astype(jnp.bfloat16).reshape(own_shape),
            mult(neighbours, attn_low[1]).astype(jnp.bfloat16).reshape(far_shape),
        ],
        axis=1,
    )
    values = jnp.concatenate(
        [
            mult(normed, attn_low[2]).astype(jnp.bfloat16).reshape(own_shape),
            mult(neighbours, attn_low[2]).astype(jnp.bfloat16).reshape(far_shape),
        ],
        axis=1,
    )
    scores = jnp.einsum("gqhd,gkhd->ghqk", quest, keys, preferred_element_type=jnp.float32) * 0.125
    allowed = jnp.concatenate([jnp.ones((images, P_SIZE), jnp.int32), nbr_valid], axis=1) > 0
    scores = jnp.where(allowed[:, None, None, :], scores, -1e30)
    top = jnp.max(scores, axis=-1, keepdims=True)
    powers = jnp.exp(scores - top)
    probs = powers / jnp.sum(powers, axis=-1, keepdims=True)
    probs_low = probs.astype(jnp.bfloat16)
    mixed = jnp.einsum("ghqk,gkhd->gqhd", probs_low, values, preferred_element_type=jnp.float32)
    mixed = mixed.reshape(images * P_SIZE, width).astype(jnp.bfloat16)
    attended = lax.psum(mult_right_t(mixed, attn_low[3]), "mp")
    middle = tokens + attended
    normed_two_f, normal_two, scale_two = layer_norm(middle, norms[2], norms[3])
    normed_two = normed_two_f.astype(jnp.bfloat16)
    inner = mult(normed_two, mlp_low[0])
    hidden = jax.nn.gelu(inner, approximate=False).astype(jnp.bfloat16)
    output = middle + lax.psum(mult_right_t(hidden, mlp_low[1]).astype(jnp.bfloat16), "mp").astype(
        jnp.float32
    )
    kept = (
        normed,
        normal_one,
        scale_one,
        quest,
        keys,
        values,
        probs,
        probs_low,
        mixed,
        normed_two,
        normal_two,
        scale_two,
        inner,
        hidden,
    )
    return (output, kept)


def renew_basis(basis):
    factor = jnp.linalg.cholesky(product(basis.T, basis))
    return jax.scipy.linalg.solve_triangular(factor, basis.T, lower=True).T


def gram_energy(grad):
    if grad.shape[0] <= grad.shape[1]:
        gram = product(grad, grad.T)
    else:
        gram = product(grad.T, grad)
    return jnp.sqrt(jnp.sum(gram * gram)) + 1e-06


def rotate_update(grad, weight, first, second, left, right):
    turned = product(product(left.T, grad), right)
    first_new = BETA_FIRST * first + (1.0 - BETA_FIRST) * turned
    second_new = BETA_SECOND * second + (1.0 - BETA_SECOND) * turned * turned
    direction = (
        first_new
        / (1.0 - BETA_FIRST**STEP)
        / (jnp.sqrt(second_new / (1.0 - BETA_SECOND**STEP)) + EPSILON)
    )
    weight_new = weight * (1.0 - RATE_MATRIX * DECAY_RATE) - RATE_MATRIX * product(
        product(left, direction), right.T
    )
    energy = gram_energy(grad)
    left_new = renew_basis(left + TURN_RATE * product(grad, product(grad.T, left)) / energy)
    right_new = renew_basis(right + TURN_RATE * product(grad.T, product(grad, right)) / energy)
    return (weight_new, first_new, second_new, left_new, right_new)


def body(
    tokens,
    cotangent,
    queue,
    nbr_index,
    nbr_valid,
    norm_params,
    norm_first,
    norm_second,
    attn_weight,
    mlp_weight,
    attn_first,
    attn_second,
    mlp_first,
    mlp_second,
    attn_left,
    attn_right,
    mlp_left,
    mlp_right,
):
    attn_low = attn_weight.astype(jnp.bfloat16)
    mlp_low = mlp_weight.astype(jnp.bfloat16)
    tokens_f = tokens.astype(jnp.float32)
    neighbours = fetch_rows(queue, nbr_index)
    output, kept = forward(tokens_f, norm_params, attn_low, mlp_low, neighbours, nbr_valid)
    again = lax.optimization_barrier((tokens_f, attn_low, mlp_low, queue, nbr_index))
    neighbours = fetch_rows(again[3], again[4])
    unused, kept = forward(again[0], norm_params, again[1], again[2], neighbours, nbr_valid)
    (
        normed,
        normal_one,
        scale_one,
        quest,
        keys,
        values,
        probs,
        probs_low,
        mixed,
        normed_two,
        normal_two,
        scale_two,
        inner,
        hidden,
    ) = kept
    images = nbr_valid.shape[0]
    width = attn_low.shape[2]
    grad_hidden = mult(cotangent, mlp_low[1])
    grad_w_two = mult_left_t(cotangent, hidden)
    unused_value, gelu_pull = jax.vjp(lambda value: jax.nn.gelu(value, approximate=False), inner)
    grad_inner = gelu_pull(grad_hidden)[0].astype(jnp.bfloat16)
    grad_w_one = mult_left_t(normed_two, grad_inner)
    grad_normed_two = lax.psum(mult_right_t(grad_inner, mlp_low[0]), "mp")
    grad_middle = cotangent.astype(jnp.float32) + norm_back(
        grad_normed_two, normal_two, scale_two, norm_params[2]
    )
    norm_two = jnp.stack(
        [jnp.sum(grad_normed_two * normal_two, axis=0), jnp.sum(grad_normed_two, axis=0)]
    )
    mlp_grad = jnp.stack([grad_w_one, grad_w_two])
    grad_middle_low = grad_middle.astype(jnp.bfloat16)
    grad_w_out = mult_left_t(grad_middle_low, mixed)
    grad_mixed = mult(grad_middle_low, attn_low[3]).astype(jnp.bfloat16)
    grad_mixed = grad_mixed.reshape(images, P_SIZE, width // HEAD, HEAD)
    grad_probs = jnp.einsum(
        "gqhd,gkhd->ghqk", grad_mixed, values, preferred_element_type=jnp.float32
    )
    grad_values = jnp.einsum(
        "ghqk,gqhd->gkhd", probs_low, grad_mixed, preferred_element_type=jnp.float32
    ).astype(jnp.bfloat16)
    grad_scores = (
        probs * (grad_probs - jnp.sum(grad_probs * probs, axis=-1, keepdims=True))
    ).astype(jnp.bfloat16)
    grad_query = (
        (
            jnp.einsum("ghqk,gkhd->gqhd", grad_scores, keys, preferred_element_type=jnp.float32)
            * 0.125
        )
        .astype(jnp.bfloat16)
        .reshape(images * P_SIZE, width)
    )
    grad_keys = (
        jnp.einsum("ghqk,gqhd->gkhd", grad_scores, quest, preferred_element_type=jnp.float32)
        * 0.125
    ).astype(jnp.bfloat16)
    key_own = grad_keys[:, :P_SIZE].reshape(images * P_SIZE, width)
    key_far = grad_keys[:, P_SIZE:].reshape(images * NBR, width)
    value_own = grad_values[:, :P_SIZE].reshape(images * P_SIZE, width)
    value_far = grad_values[:, P_SIZE:].reshape(images * NBR, width)
    grad_w_query = mult_left_t(normed, grad_query)
    grad_w_key = mult_left_t(normed, key_own) + mult_left_t(neighbours, key_far)
    grad_w_value = mult_left_t(normed, value_own) + mult_left_t(neighbours, value_far)
    attn_grad = jnp.stack([grad_w_query, grad_w_key, grad_w_value, grad_w_out])
    grad_normed = lax.psum(
        mult_right_t(grad_query, attn_low[0])
        + mult_right_t(key_own, attn_low[1])
        + mult_right_t(value_own, attn_low[2]),
        "mp",
    )
    input_grad = grad_middle + norm_back(grad_normed, normal_one, scale_one, norm_params[0])
    norm_one = jnp.stack([jnp.sum(grad_normed * normal_one, axis=0), jnp.sum(grad_normed, axis=0)])
    attn_grad, mlp_grad, norm_one, norm_two = lax.psum(
        (attn_grad, mlp_grad, norm_one, norm_two), "dp"
    )
    norm_grad = jnp.concatenate([norm_one, norm_two], axis=0)
    norm_first_new = BETA_FIRST * norm_first + (1.0 - BETA_FIRST) * norm_grad
    norm_second_new = BETA_SECOND * norm_second + (1.0 - BETA_SECOND) * norm_grad * norm_grad
    norm_new = norm_params - RATE_NORM * (norm_first_new / (1.0 - BETA_FIRST**STEP)) / (
        jnp.sqrt(norm_second_new / (1.0 - BETA_SECOND**STEP)) + EPSILON
    )
    attn_made = [
        rotate_update(
            attn_grad[slot],
            attn_weight[slot],
            attn_first[slot],
            attn_second[slot],
            attn_left[slot],
            attn_right[slot],
        )
        for slot in range(4)
    ]
    mlp_made = [
        rotate_update(
            mlp_grad[slot],
            mlp_weight[slot],
            mlp_first[slot],
            mlp_second[slot],
            mlp_left[slot],
            mlp_right[slot],
        )
        for slot in range(2)
    ]
    attn_new, attn_first_new, attn_second_new, attn_left_new, attn_right_new = (
        jnp.stack([entry[index] for entry in attn_made]) for index in range(5)
    )
    mlp_new, mlp_first_new, mlp_second_new, mlp_left_new, mlp_right_new = (
        jnp.stack([entry[index] for entry in mlp_made]) for index in range(5)
    )
    return (
        output.astype(jnp.bfloat16),
        input_grad,
        norm_grad,
        attn_grad,
        mlp_grad,
        norm_first_new,
        norm_second_new,
        norm_new,
        attn_first_new,
        attn_second_new,
        mlp_first_new,
        mlp_second_new,
        attn_left_new,
        attn_right_new,
        mlp_left_new,
        mlp_right_new,
        attn_new,
        attn_new.astype(jnp.bfloat16),
        mlp_new,
        mlp_new.astype(jnp.bfloat16),
    )


def solution(mesh):
    return jax.shard_map(
        body,
        mesh=mesh,
        in_specs=(
            P("dp", None),
            P("dp", None),
            P("dp", None),
            P("dp", None),
            P("dp", None),
            P(),
            P(),
            P(),
            P(None, None, "mp"),
            P(None, None, "mp"),
            P(None, None, "mp"),
            P(None, None, "mp"),
            P(None, None, "mp"),
            P(None, None, "mp"),
            P(None, "mp", None),
            P(None, "mp", None),
            P(None, "mp", None),
            P(None, "mp", None),
        ),
        out_specs=(
            P("dp", None),
            P("dp", None),
            P(),
            P(None, None, "mp"),
            P(None, None, "mp"),
            P(),
            P(),
            P(),
            P(None, None, "mp"),
            P(None, None, "mp"),
            P(None, None, "mp"),
            P(None, None, "mp"),
            P(None, "mp", None),
            P(None, "mp", None),
            P(None, "mp", None),
            P(None, "mp", None),
            P(None, None, "mp"),
            P(None, None, "mp"),
            P(None, None, "mp"),
            P(None, None, "mp"),
        ),
        check_vma=False,
    )
```

profile of v0, /device:TPU:0, one launch (start us, length us, event | category | flops | bytes accessed | tf_op | source)
XLA Modules:
  0.0 2095.4 jit_solution(3212570436003005472)
XLA Ops:
  40.5 31.1 %all-gather.5.cloned.1.call-done = bf16[2048,384]{1,0:T(8,128)(2,1)} async-done(((bf16[128,384]{1,0:T(8,128)(2,1)}), bf16[2048,384]{1,0:T(8,128)(2,1)}) %all-gather.5.cloned.1.call-update) | async-done | bytes 1572880 | tf_op jit(solution)/shard_map/all_gather | solution.py:59
  89.6 20.3 all-reduce.17.cloned.1.call-done
  124.9 14.4 add_convert_fusion
  208.2 20.3 all-gather.3.cloned.1.call-done
  244.5 144.3 %all-reduce.21.cloned.1.call-done = (f32[4,384,192]{1,2,0:T(8,128)}, f32[2,384,768]{2,1,0:T(8,128)}) async-done(((f32[4,384,192]{1,2,0:T(8,128)}, f32[2,384,768]{2,1,0:T(8,128)}), (f32[4,384,192]{1,2,0:T(8,128)}, f32[2,384,768]{2,1,0:T(8,128)})) %all-reduce.21.cloned.1.call-update) | async-done | bytes 3538960 | tf_op jit(solution)/shard_map/psum | solution.py:256
  511.7 11.9 cholesky.1228
  557.6 11.9 cholesky.1190
  686.2 29.7 %custom-call.109 = f32[3,128,128]{1,2,0:T(8,128)S(1)} custom-call(f32[3,128,128]{2,1,0:T(8,128)S(1)} %get-tuple-element.131), custom_call_target="InvertDiagBlocksLowerTriangular" | custom-call | tf_op jit(solution)/shard_map/jit(_solve_triangular)/triangular_solve | solution.py:127
  752.1 12.1 cholesky.1118
  803.4 29.7 %custom-call.106 = f32[3,128,128]{1,2,0:T(8,128)S(1)} custom-call(f32[3,128,128]{2,1,0:T(8,128)S(1)} %get-tuple-element.130), custom_call_target="InvertDiagBlocksLowerTriangular" | custom-call | tf_op jit(solution)/shard_map/jit(_solve_triangular)/triangular_solve | solution.py:127
  869.3 11.9 cholesky.1076
  920.5 29.9 %custom-call.103 = f32[3,128,128]{1,2,0:T(8,128)S(1)} custom-call(f32[3,128,128]{2,1,0:T(8,128)S(1)} %get-tuple-element.129), custom_call_target="InvertDiagBlocksLowerTriangular" | custom-call | tf_op jit(solution)/shard_map/jit(_solve_triangular)/triangular_solve | solution.py:127
  986.5 11.9 cholesky.1034
  1037.7 29.7 %custom-call.100 = f32[3,128,128]{1,2,0:T(8,128)S(1)} custom-call(f32[3,128,128]{2,1,0:T(8,128)S(1)} %get-tuple-element.128), custom_call_target="InvertDiagBlocksLowerTriangular" | custom-call | tf_op jit(solution)/shard_map/jit(_solve_triangular)/triangular_solve | solution.py:127
  1079.5 21.1 %custom-call.117 = f32[2,128,128]{1,2,0:T(8,128)} custom-call(f32[2,128,128]{2,1,0:T(8,128)} %pad_maximum_fusion.21), custom_call_target="InvertDiagBlocksLowerTriangular" | custom-call | tf_op jit(solution)/shard_map/jit(_solve_triangular)/triangular_solve | solution.py:127
  1105.3 20.3 custom-call.115
  1129.4 19.7 custom-call.113
  1152.1 20.1 custom-call.111
  1210.4 11.9 cholesky.1396
  1261.6 29.7 %custom-call.123 = f32[3,128,128]{1,2,0:T(8,128)S(1)} custom-call(f32[3,128,128]{2,1,0:T(8,128)S(1)} %get-tuple-element.133), custom_call_target="InvertDiagBlocksLowerTriangular" | custom-call | tf_op jit(solution)/shard_map/jit(_solve_triangular)/triangular_solve | solution.py:127
  1332.4 12.2 cholesky.1354
  1383.9 29.7 %custom-call.120 = f32[3,128,128]{1,2,0:T(8,128)S(1)} custom-call(f32[3,128,128]{2,1,0:T(8,128)S(1)} %get-tuple-element.132), custom_call_target="InvertDiagBlocksLowerTriangular" | custom-call | tf_op jit(solution)/shard_map/jit(_solve_triangular)/triangular_solve | solution.py:127
  1522.6 12.1 cholesky.1587
  1572.5 11.9 cholesky.1615
  1596.1 17.4 while.28
  1614.2 59.8 %custom-call.135 = f32[6,128,128]{1,2,0:T(8,128)S(1)} custom-call(f32[6,128,128]{2,1,0:T(8,128)} %copy-done.105), custom_call_target="InvertDiagBlocksLowerTriangular" | custom-call | tf_op jit(solution)/shard_map/jit(_solve_triangular)/triangular_solve | solution.py:127
  1784.3 12.2 cholesky.1485
  1831.2 11.9 cholesky.1513
  1853.2 21.1 %while.27 = (s32[]{:T(128)}, f32[768,768]{1,0:T(8,128)}, s32[6,2]{0,1:T(2,128)S(1)}, f32[6,128,128]{2,1,0:T(8,128)}, s32[]{:T(128)}) while((s32[]{:T(128)}, f32[768,768]{1,0:T(8,128)}, s32[6,2]{0,1:T(2,128)S(1)}, f32[6,128,128]{2,1,0:T(8,128)}, s32[]{:T(128)}) %tuple.320), condition=%wide.while_cond.2, body=%wide.while_body.2.sunk | while | flops 2 | bytes 132205 | solution.py:127
  1874.2 59.9 %custom-call.129 = f32[6,128,128]{1,2,0:T(8,128)S(1)} custom-call(f32[6,128,128]{2,1,0:T(8,128)} %get-tuple-element.134), custom_call_target="InvertDiagBlocksLowerTriangular" | custom-call | tf_op jit(solution)/shard_map/jit(_solve_triangular)/triangular_solve | solution.py:127
  2017.2 15.5 convolution_convert_fusion
  2035.8 40.3 %all-reduce.6 = (f32[2,384]{1,0:T(2,128)S(1)}, f32[2,384]{1,0:T(2,128)S(1)}) all-reduce(f32[2,384]{1,0:T(2,128)S(1)} %copy-done.129, f32[2,384]{1,0:T(2,128)S(1)} %pad_maximum_fusion.23), channel_id=1, replica_groups=mesh['dp'=16,'mp'=2] {'dp'}, use_global_device_ids=true, to_apply=%region_27.28 | all-reduce | flops 1536 | bytes 12288 | tf_op jit(solution)/shard_map/psum | solution.py:256
  (956 shorter events, 1303.2 us)
Async XLA Ops:
  7.2 64.4 %all-gather.5.cloned.1.call-start = ((), (), s32[]{:S(2)}) async-start(), calls=%async_computation.2 | async-start | bytes 1671168 | tf_op jit(solution)/shard_map/all_gather | solution.py:59
  9.6 100.3 %copy-start = (f32[1576,384]{1,0:T(8,128)}, f32[1576,384]{1,0:T(8,128)S(1)}, u32[]{:S(2)}) copy-start(f32[1576,384]{1,0:T(8,128)S(1)} %convert_element_type.139) | copy-start | bytes 7262212
  10.9 99.1 %all-reduce.17.cloned.1.call-start = ((), (), s32[]{:S(2)}) async-start(), calls=%async_computation.3 | async-start | bytes 4841472 | tf_op jit(solution)/shard_map/psum | solution.py:97
  11.9 159.8 %copy-start.115 = (f32[384]{0:T(512)}, f32[384]{0:T(512)S(1)}, u32[]{:S(2)}) copy-start(f32[384]{0:T(512)S(1)} %get-tuple-element.185) | copy-start | bytes 4612
  89.3 78.8 %all-reduce.19.cloned.1.call-start = ((), (), s32[]{:S(2)}) async-start(), calls=%async_computation.4 | async-start | bytes 4841472 | tf_op jit(solution)/shard_map/psum | solution.py:207
  143.8 84.8 %all-gather.3.cloned.1.call-start = ((), (), s32[]{:S(2)}) async-start(), calls=%async_computation | async-start | bytes 1671168 | tf_op jit(solution)/shard_map/all_gather | solution.py:59
  144.4 244.4 %all-reduce.21.cloned.1.call-start = ((), (), s32[]{:S(2)}) async-start(), calls=%async_computation.5 | async-start | bytes 7077888 | tf_op jit(solution)/shard_map/psum | solution.py:256
  208.1 20.4 copy-start.135
  208.1 23.3 %copy-start.61 = (bf16[8,197,3,64]{1,3,2,0:T(8,128)(2,1)S(1)}, bf16[8,197,3,64]{1,3,2,0:T(8,128)(2,1)}, u32[]{:S(2)}) copy-start(bf16[8,197,3,64]{1,3,2,0:T(8,128)(2,1)} %copy.89) | copy-start | bytes 1815556
  208.1 23.3 %copy-start.62 = (bf16[8,197,3,64]{1,0,3,2:T(8,128)(2,1)S(1)}, bf16[8,197,3,64]{1,0,3,2:T(8,128)(2,1)}, u32[]{:S(2)}) copy-start(bf16[8,197,3,64]{1,0,3,2:T(8,128)(2,1)} %reshape.285) | copy-start | bytes 1815556
  208.1 1805.6 %all-reduce.23.cloned.1.call-start = ((), (), s32[]{:S(2)}) async-start(), calls=%async_computation.6 | async-start | bytes 9682944 | tf_op jit(solution)/shard_map/psum | solution.py:97
  244.3 1836.5 %all-reduce.15.cloned.1.call-start = ((), (), s32[]{:S(2)}) async-start(), calls=%async_computation.1 | async-start | bytes 2420736 | tf_op jit(solution)/shard_map/psum | solution.py:103
  396.0 19.2 copy-start.81
  435.6 28.4 %copy-start.75 = (f32[384,192]{1,0:T(8,128)S(1)}, f32[384,192]{1,0:T(8,128)}, u32[]{:S(2)}) copy-start(f32[384,192]{1,0:T(8,128)} %fusion.324) | copy-start | bytes 884740
  479.8 28.3 %copy-start.74 = (f32[384,192]{1,0:T(8,128)S(1)}, f32[384,192]{1,0:T(8,128)}, u32[]{:S(2)}) copy-start(f32[384,192]{1,0:T(8,128)} %fusion.323) | copy-start | bytes 884740
  534.1 66.6 %slice-start = ((s8[4718592]{0:T(1024)(128)(4,1)}), s8[524288]{0:T(1024)(128)(4,1)S(1)}, s32[]{:S(2)}) async-start(s8[4718592]{0:T(1024)(128)(4,1)} %bitcast.1062), calls=%async_computation.7 | async-start | bytes 1048576
  609.6 67.9 %copy-start.139 = (s32[3]{0:T(128)S(1)}, s32[3]{0:T(128)}, u32[]{:S(2)}) copy-start(s32[3]{0:T(128)} %iota_multiply_fusion.1) | copy-start | bytes 40
  621.4 94.6 %copy-start.42 = (f32[384,384]{1,0:T(8,128)S(1)}, f32[384,384]{1,0:T(8,128)}, u32[]{:S(2)}) copy-start(f32[384,384]{1,0:T(8,128)} %fusion.95) | copy-start | bytes 1769476
  738.4 94.8 %copy-start.40 = (f32[384,384]{1,0:T(8,128)S(1)}, f32[384,384]{1,0:T(8,128)}, u32[]{:S(2)}) copy-start(f32[384,384]{1,0:T(8,128)} %fusion.97) | copy-start | bytes 1769476
  855.6 94.8 %copy-start.39 = (f32[384,384]{1,0:T(8,128)S(1)}, f32[384,384]{1,0:T(8,128)}, u32[]{:S(2)}) copy-start(f32[384,384]{1,0:T(8,128)} %fusion.99) | copy-start | bytes 1769476
  972.8 94.6 %copy-start.38 = (f32[384,384]{1,0:T(8,128)S(1)}, f32[384,384]{1,0:T(8,128)}, u32[]{:S(2)}) copy-start(f32[384,384]{1,0:T(8,128)} %fusion.101) | copy-start | bytes 1769476
  1074.7 25.9 %copy-start.54 = (f32[192,192]{1,0:T(8,128)S(1)}, f32[192,192]{1,0:T(8,128)}, u32[]{:S(2)}) copy-start(f32[192,192]{1,0:T(8,128)} %copy-done.53) | copy-start | bytes 442372
  1074.7 50.8 %copy-start.56 = (f32[192,192]{1,0:T(8,128)S(1)}, f32[192,192]{1,0:T(8,128)}, u32[]{:S(2)}) copy-start(f32[192,192]{1,0:T(8,128)} %copy-done.55) | copy-start | bytes 442372
  1077.9 71.2 %copy-start.58 = (f32[192,192]{1,0:T(8,128)S(1)}, f32[192,192]{1,0:T(8,128)}, u32[]{:S(2)}) copy-start(f32[192,192]{1,0:T(8,128)} %copy-done.57) | copy-start | bytes 442372
  1078.0 51.4 %copy-start.106 = (f32[1,128,128]{2,1,0:T(8,128)S(1)}, f32[1,128,128]{2,1,0:T(8,128)}, u32[]{:S(2)}) copy-start(f32[1,128,128]{2,1,0:T(8,128)} %slice_bitcast_fusion.105) | copy-start | bytes 196612
  1078.0 94.2 %copy-start.60 = (f32[192,192]{1,0:T(8,128)S(1)}, f32[192,192]{1,0:T(8,128)}, u32[]{:S(2)}) copy-start(f32[192,192]{1,0:T(8,128)} %copy-done.59) | copy-start | bytes 442372
  1596.0 99.0 %slice-start.2 = ((s8[4718592]{0:T(1024)(128)(4,1)}), s8[524288]{0:T(1024)(128)(4,1)S(1)}, s32[]{:S(2)}) async-start(s8[4718592]{0:T(1024)(128)(4,1)} %bitcast.1064), calls=%async_computation.9 | async-start | bytes 1048576
  1874.2 64.9 %copy-start.18 = (f32[768,768]{1,0:T(8,128)S(1)}, f32[768,768]{1,0:T(8,128)}, u32[]{:S(2)}) copy-start(f32[768,768]{1,0:T(8,128)} %copy-done.17) | copy-start | bytes 7077892
  2017.2 15.6 copy-start.1
  2032.8 43.3 %copy-start.126 = (f32[4,384]{1,0:T(4,128)S(1)}, f32[4,384]{1,0:T(4,128)}, u32[]{:S(2)}) copy-start(f32[4,384]{1,0:T(4,128)} %param.36) | copy-start | bytes 18436
  2032.8 43.3 %copy-start.132 = (f32[4,384]{1,0:T(4,128)S(1)}, f32[4,384]{1,0:T(4,128)}, u32[]{:S(2)}) copy-start(f32[4,384]{1,0:T(4,128)} %param.38) | copy-start | bytes 18436
  2032.8 43.3 %copy-start.133 = (f32[4,384]{1,0:T(4,128)S(1)}, f32[4,384]{1,0:T(4,128)}, u32[]{:S(2)}) copy-start(f32[4,384]{1,0:T(4,128)} %param.37) | copy-start | bytes 18436
  (121 other events, 463.2 us)
Sparse Core Ops, SparseCore 0:
  11.0 60.5 all-gather.4
  89.5 20.4 all-reduce.16
  143.9 22.8 all-reduce.18
  169.5 59.0 all-gather.2
  234.9 153.8 all-reduce.20
  392.0 28.4 all-reduce.22
  2032.9 18.9 all-reduce.14
where the time goes:
time: 2110 us; the launch traced here: 2100 us
  other arithmetic  1200 us (57%)
  matrix products  385 us (18%)
  waiting for transfers between devices  217 us (10%)
  local copies, waits for them, and re-layouts  204 us (10%)
  between operations  46.5 us (2%)
  blocking collectives  40.3 us (2%)
    another operation x140, other arithmetic, renew_basis(): factor = jnp.linalg.cholesky(product(basis.T, basis))  720 us
    another operation x33, other arithmetic, renew_basis(): return jax.scipy.linalg.solve_triangular(factor, basis.T, lower=True).T  400 us
    dot_general x60, matrix products, product(): return jnp.dot(left, right, precision=lax.Precision.HIGHEST)  152 us
    psum x1, waiting for transfers between devices, body(): lax.psum((attn_grad, mlp_grad, norm_one, norm_two), 'dp')  144 us
    another operation x108, local copies, waits for them, and re-layouts, renew_basis(): return jax.scipy.linalg.solve_triangular(factor, basis.T, lower=True).T  95.8 us
    another operation x64, matrix products, renew_basis(): return jax.scipy.linalg.solve_triangular(factor, basis.T, lower=True).T  76.1 us
    another operation x52, matrix products, renew_basis(): factor = jnp.linalg.cholesky(product(basis.T, basis))  61.8 us
    all_gather x2, waiting for transfers between devices, fetch_rows(): piece = lax.all_gather(queue, 'dp', axis=0, tiled=True)  51.5 us
  transfers between devices with their start and end apart: 7, of which 4 were waited for; matrix products, arithmetic and copies ran while one was open for 80% of the time, Pallas kernels for 0%

commit v1 on v0

--- a/solution.py
+++ b/solution.py
@@ -1,6 +1,8 @@
 import jax
 import jax.numpy as jnp
 from jax import lax
+from jax.experimental import pallas as pl
+from jax.experimental.pallas import tpu as pltpu
 from jax.sharding import PartitionSpec as P
 
 P_SIZE = 197
@@ -122,35 +124,207 @@
     return (output, kept)
 
 
-def renew_basis(basis):
-    factor = jnp.linalg.cholesky(product(basis.T, basis))
-    return jax.scipy.linalg.solve_triangular(factor, basis.T, lower=True).T
-
-
-def gram_energy(grad):
-    if grad.shape[0] <= grad.shape[1]:
-        gram = product(grad, grad.T)
-    else:
-        gram = product(grad.T, grad)
-    return jnp.sqrt(jnp.sum(gram * gram)) + 1e-06
-
-
-def rotate_update(grad, weight, first, second, left, right):
-    turned = product(product(left.T, grad), right)
-    first_new = BETA_FIRST * first + (1.0 - BETA_FIRST) * turned
-    second_new = BETA_SECOND * second + (1.0 - BETA_SECOND) * turned * turned
-    direction = (
+HIGH = lax.Precision.HIGH
+HIGHEST = lax.Precision.HIGHEST
+BLOCK = 256
+NEAR = 0.01
+
+BF = jnp.bfloat16
+
+
+def dot_nn(a, b, precision=None):
+    return lax.dot_general(a, b, (((1,), (0,)), ((), ())), precision=precision, preferred_element_type=jnp.float32)
+
+
+def dot_nt(a, b, precision=None):
+    return lax.dot_general(a, b, (((1,), (1,)), ((), ())), precision=precision, preferred_element_type=jnp.float32)
+
+
+def dot_tn(a, b, precision=None):
+    return lax.dot_general(a, b, (((0,), (0,)), ((), ())), precision=precision, preferred_element_type=jnp.float32)
+
+
+def split(a):
+    high = a.astype(BF)
+    return high, (a - high.astype(jnp.float32)).astype(BF)
+
+
+def below(size):
+    row = lax.broadcasted_iota(jnp.int32, (size, size), 0)
+    col = lax.broadcasted_iota(jnp.int32, (size, size), 1)
+    return row > col, row == col
+
+
+def whiten(gram, rounds):
+    size = gram.shape[0]
+    lower, same = below(size)
+    eye = jnp.where(same, 1.0, 0.0)
+    on_diag = jnp.where(same, gram, 0.0)
+    s_col = lax.rsqrt(jnp.maximum(jnp.sum(on_diag, axis=1, keepdims=True), 1e-30))
+    s_row = lax.rsqrt(jnp.maximum(jnp.sum(on_diag, axis=0, keepdims=True), 1e-30))
+    state = gram * s_col * s_row
+    made = jnp.where(same, s_col, 0.0)
+    for turn in range(rounds):
+        under = jnp.where(lower, state, 0.0)
+        under_low = under.astype(BF)
+        moved = dot_nn(under_low, state.astype(BF))
+        mass = jnp.sum(under * under, axis=1, keepdims=True)
+        curve = jnp.sum(moved * under, axis=1, keepdims=True)
+        pace = jnp.where(curve > mass, mass / jnp.maximum(curve, 1e-30), 1.0)
+        left = 1.0 - 2.0 * pace * mass + pace * pace * curve
+        scale = lax.rsqrt(jnp.maximum(left, 1e-6))
+        step = (scale * (eye - pace * under)).astype(BF)
+        if turn + 1 < rounds:
+            state = dot_nt((scale * (state - pace * moved)).astype(BF), step)
+        made = dot_nn(step, made.astype(BF))
+    return made.astype(BF)
+
+
+def miss(gram):
+    lower, same = below(gram.shape[0])
+    return jnp.where(lower, gram, 0.0) + jnp.where(same, 0.5 * (gram - 1.0), 0.0)
+
+
+def turn_by(base, made):
+    high, low = split(base)
+    return dot_nt(high, made) + dot_nt(low, made)
+
+
+def cuts(width):
+    return [(at, min(BLOCK, width - at)) for at in range(0, width, BLOCK)]
+
+
+def renew_fast(base_ref, out_ref, rest_ref):
+    width = base_ref.shape[1]
+    worst = 0.0
+    src = base_ref
+    for at, size in cuts(width):
+        block = src[:, at:at + size]
+        low = block.astype(BF)
+        made = whiten(dot_tn(low, low), 3)
+        block = turn_by(block, made)
+        off = miss(dot_tn(block, block, HIGH))
+        worst = jnp.maximum(worst, jnp.sum(off * off) / size)
+        block = block - dot_nt(block.astype(BF), off.astype(BF))
+        out_ref[:, at:at + size] = block
+        if at + size < width:
+            rest = src[:, at + size:]
+            rest_ref[:, at + size:] = rest - dot_nn(block, dot_tn(block, rest, HIGH), HIGH)
+            src = rest_ref
+    return worst
+
+
+def renew_safe(base_ref, out_ref):
+    width = base_ref.shape[1]
+    out_ref[...] = base_ref[...]
+    for at, size in cuts(width):
+        cols = slice(at, at + size)
+
+        def again(carry, cols=cols, size=size):
+            count, unused = carry
+            block = out_ref[:, cols]
+            gram = dot_tn(block, block, HIGHEST)
+            off = miss(gram)
+            far = jnp.logical_not(jnp.sum(off * off) / size < NEAR)
+
+            @pl.when(far)
+            def _():
+                out_ref[:, cols] = turn_by(block, whiten(gram, 3))
+
+            @pl.when(jnp.logical_not(far))
+            def _():
+                out_ref[:, cols] = block - dot_nt(block, off, HIGH)
+
+            return count + 1, far
+
+        lax.while_loop(lambda carry: jnp.logical_and(carry[0] < 60, carry[1]), again, (0, True))
+        if at + size < width:
+            block = out_ref[:, cols]
+            for unused in range(2):
+                rest = out_ref[:, at + size:]
+                out_ref[:, at + size:] = rest - dot_nn(block, dot_tn(block, rest, HIGHEST), HIGHEST)
+
+
+def update_kernel(
+    grad_ref, weight_ref, first_ref, second_ref, left_ref, right_ref,
+    new_ref, copy_ref, first_new_ref, second_new_ref, left_new_ref, right_new_ref,
+    left_base, right_base, left_rest, right_rest,
+):
+    grad = grad_ref[0].astype(BF)
+    left_high, left_low = split(left_ref[0])
+    right = right_ref[0]
+    right_high = right.astype(BF)
+    half = dot_tn(left_high, grad) + dot_tn(left_low, grad)
+    turned = dot_nn(half, right, HIGH)
+    first_new = BETA_FIRST * first_ref[0] + (1.0 - BETA_FIRST) * turned
+    second_new = BETA_SECOND * second_ref[0] + (1.0 - BETA_SECOND) * turned * turned
+    first_new_ref[0] = first_new
+    second_new_ref[0] = second_new
+    move = (
         first_new
         / (1.0 - BETA_FIRST**STEP)
         / (jnp.sqrt(second_new / (1.0 - BETA_SECOND**STEP)) + EPSILON)
     )
-    weight_new = weight * (1.0 - RATE_MATRIX * DECAY_RATE) - RATE_MATRIX * product(
-        product(left, direction), right.T
-    )
-    energy = gram_energy(grad)
-    left_new = renew_basis(left + TURN_RATE * product(grad, product(grad.T, left)) / energy)
-    right_new = renew_basis(right + TURN_RATE * product(grad.T, product(grad, right)) / energy)
-    return (weight_new, first_new, second_new, left_new, right_new)
+    back = dot_nn(left_high, move.astype(BF)).astype(BF)
+    new = weight_ref[0] * (1.0 - RATE_MATRIX * DECAY_RATE) - RATE_MATRIX * dot_nt(back, right_high)
+    new_ref[0] = new
+    copy_ref[0] = new.astype(BF)
+
+    if grad.shape[0] <= grad.shape[1]:
+        gram = dot_nt(grad, grad)
+        energy = jnp.sqrt(jnp.sum(gram * gram)) + 1e-06
+        pace = TURN_RATE / energy
+        left_base[...] = left_ref[0] + dot_nn(gram.astype(BF), left_high) * pace
+        right_base[...] = right + dot_tn(grad, dot_nn(grad, right_high).astype(BF)) * pace
+    else:
+        gram = dot_tn(grad, grad)
+        energy = jnp.sqrt(jnp.sum(gram * gram)) + 1e-06
+        pace = TURN_RATE / energy
+        left_base[...] = left_ref[0] + dot_nn(grad, dot_tn(grad, left_high).astype(BF)) * pace
+        right_base[...] = right + dot_nn(gram.astype(BF), right_high) * pace
+
+    worst_left = renew_fast(left_base, left_new_ref.at[0], left_rest)
+    worst_right = renew_fast(right_base, right_new_ref.at[0], right_rest)
+
+    @pl.when(jnp.logical_not(worst_left < NEAR))
+    def _():
+        renew_safe(left_base, left_new_ref.at[0])
+
+    @pl.when(jnp.logical_not(worst_right < NEAR))
+    def _():
+        renew_safe(right_base, right_new_ref.at[0])
+
+
+def update_stack(grad, weight, first, second, left, right):
+    slots, rows, width = grad.shape
+
+    def spec(shape):
+        return pl.BlockSpec((1,) + shape, lambda slot: (slot, 0, 0))
+
+    flat = spec((rows, width))
+    f32 = jnp.float32
+    return pl.pallas_call(
+        update_kernel,
+        grid=(slots,),
+        in_specs=[flat] * 4 + [spec((rows, rows)), spec((width, width))],
+        out_specs=[flat] * 4 + [spec((rows, rows)), spec((width, width))],
+        out_shape=[
+            jax.ShapeDtypeStruct(weight.shape, f32),
+            jax.ShapeDtypeStruct(weight.shape, BF),
+            jax.ShapeDtypeStruct(weight.shape, f32),
+            jax.ShapeDtypeStruct(weight.shape, f32),
+            jax.ShapeDtypeStruct(left.shape, f32),
+            jax.ShapeDtypeStruct(right.shape, f32),
+        ],
+        scratch_shapes=[
+            pltpu.VMEM((rows, rows), f32),
+            pltpu.VMEM((width, width), f32),
+            pltpu.VMEM((rows, rows), f32),
+            pltpu.VMEM((width, width), f32),
+        ],
+        compiler_params=pltpu.CompilerParams(vmem_limit_bytes=60 * 1024 * 1024),
+        name="rotated_update_%d" % width,
+    )(grad, weight, first, second, left, right)
 
 
 def body(
@@ -262,33 +436,22 @@
     norm_new = norm_params - RATE_NORM * (norm_first_new / (1.0 - BETA_FIRST**STEP)) / (
         jnp.sqrt(norm_second_new / (1.0 - BETA_SECOND**STEP)) + EPSILON
     )
-    attn_made = [
-        rotate_update(
-            attn_grad[slot],
-            attn_weight[slot],
-            attn_first[slot],
-            attn_second[slot],
-            attn_left[slot],
-            attn_right[slot],
-        )
-        for slot in range(4)
-    ]
-    mlp_made = [
-        rotate_update(
-            mlp_grad[slot],
-            mlp_weight[slot],
-            mlp_first[slot],
-            mlp_second[slot],
-            mlp_left[slot],
-            mlp_right[slot],
-        )
-        for slot in range(2)
-    ]
-    attn_new, attn_first_new, attn_second_new, attn_left_new, attn_right_new = (
-        jnp.stack([entry[index] for entry in attn_made]) for index in range(5)
-    )
-    mlp_new, mlp_first_new, mlp_second_new, mlp_left_new, mlp_right_new = (
-        jnp.stack([entry[index] for entry in mlp_made]) for index in range(5)
+    def flip(value):
+        return value.transpose(0, 2, 1)
+
+    attn_new, attn_copy, attn_first_new, attn_second_new, attn_right_new, attn_left_new = update_stack(
+        flip(attn_grad),
+        flip(attn_weight),
+        flip(attn_first),
+        flip(attn_second),
+        attn_right,
+        attn_left,
+    )
+    attn_new, attn_copy, attn_first_new, attn_second_new = map(
+        flip, (attn_new, attn_copy, attn_first_new, attn_second_new)
+    )
+    mlp_new, mlp_copy, mlp_first_new, mlp_second_new, mlp_left_new, mlp_right_new = update_stack(
+        mlp_grad, mlp_weight, mlp_first, mlp_second, mlp_left, mlp_right
     )
     return (
         output.astype(jnp.bfloat16),
@@ -308,9 +471,9 @@
         mlp_left_new,
         mlp_right_new,
         attn_new,
-        attn_new.astype(jnp.bfloat16),
+        attn_copy,
         mlp_new,
-        mlp_new.astype(jnp.bfloat16),
+        mlp_copy,
     )
 
 

time: 2110 us -> 590 us (0.28)
  other arithmetic: 1200 us -> 47.3 us
  matrix products: 385 us -> 84.7 us
  local copies, waits for them, and re-layouts: 204 us -> 59.2 us
  Pallas kernels: 0 us -> 119 us
  between operations: 46.5 us -> 15.4 us
    another operation x193 -> x0, other arithmetic: 1140 us -> none  [the longest x140 720 us: renew_basis(): factor = jnp.linalg.cholesky(product(basis.T, basis))]
    dot_general x60 -> x0, matrix products: 152 us -> none  [product(): return jnp.dot(left, right, precision=lax.Precision.HIGHEST)]
    another operation x116 -> x0, matrix products: 138 us -> none  [the longest x64 76.1 us: renew_basis(): return jax.scipy.linalg.solve_triangular(factor, basis.T, lower=True).T]
    pallas_call x0 -> x2, Pallas kernels: none -> 119 us  [update_stack(): pl.pallas_call(update_kernel, grid=(slots,), in_specs=[flat] * 4 + [spec(...]
    another operation x146 -> x0, local copies, waits for them, and re-layouts: 103 us -> none  [the longest x108 95.8 us: renew_basis(): return jax.scipy.linalg.solve_triangular(factor, basis.T, lower=True).T]
    unnamed x297 -> x128, local copies, waits for them, and re-layouts: 43.6 us -> 13.4 us
  transfers between devices with their start and end apart: 7 -> 7, of which waited for: 4 -> 4; matrix products, arithmetic and copies ran while one was open for 80% -> 20% of each run, Pallas kernels for 0% -> 21%
where the time goes in v1:
time: 590 us; the launch traced here: 581 us
  waiting for transfers between devices  214 us (36%)
  Pallas kernels  119 us (20%)
  matrix products  84.7 us (14%)
  local copies, waits for them, and re-layouts  59.2 us (10%)
  other arithmetic  47.3 us (8%)
  blocking collectives  40.2 us (7%)
  between operations  15.4 us (3%)
    psum x1, waiting for transfers between devices, body(): lax.psum((attn_grad, mlp_grad, norm_one, norm_two), 'dp')  144 us
    pallas_call x2, Pallas kernels, update_stack(): pl.pallas_call(update_kernel, grid=(slots,), in_specs=[flat] * 4 + [spec(...  119 us
    all_gather x2, waiting for transfers between devices, fetch_rows(): piece = lax.all_gather(queue, 'dp', axis=0, tiled=True)  48.8 us
    psum x1, blocking collectives, body(): lax.psum((attn_grad, mlp_grad, norm_one, norm_two), 'dp')  40.2 us
    dot_general x15, matrix products, mult(): return jnp.dot(left, right, preferred_element_type=jnp.float32)  29.9 us
    dot_general x7, matrix products, mult_right_t(): lax.dot_general(left, right, (((1,), (1,)), ((), ())), preferred_element_...  27.1 us
    psum x2, waiting for transfers between devices, forward(): attended = lax.psum(mult_right_t(mixed, attn_low[3]), 'mp')  20.4 us
    unnamed x128, local copies, waits for them, and re-layouts  13.4 us
  transfers between devices with their start and end apart: 7, of which 4 were waited for; matrix products, arithmetic and copies ran while one was open for 20% of the time, Pallas kernels for 21%

profile of v1, /device:TPU:0, one launch (start us, length us, event | category | flops | bytes accessed | tf_op | source)
XLA Modules:
  0.0 580.5 jit_solution(9901619933921409925)
XLA Ops:
  8.6 2.8 convert_element_type.147
  23.0 3.1 reshape.173
  28.3 2.7 convolution_convert_fusion.3
  31.0 3.1 reshape.172
  34.1 2.7 convolution_convert_fusion.4
  36.8 3.1 reshape.170
  42.8 30.8 %all-gather.5.cloned.1.call-done = bf16[2048,384]{1,0:T(8,128)(2,1)} async-done(((bf16[128,384]{1,0:T(8,128)(2,1)}), bf16[2048,384]{1,0:T(8,128)(2,1)}) %all-gather.5.cloned.1.call-update) | async-done | bytes 1572880 | tf_op jit(solution)/shard_map/all_gather | solution.py:61
  79.5 2.5 fusion.131
  85.6 2.6 convert_element_type.163
  88.1 3.1 fusion.71
  91.5 20.4 %all-reduce.12.cloned.1.call-done = f32[1576,384]{1,0:T(8,128)} async-done(((f32[1576,384]{1,0:T(8,128)}), f32[1576,384]{1,0:T(8,128)}) %all-reduce.12.cloned.1.call-update) | async-done | bytes 2420752 | tf_op jit(solution)/shard_map/psum | solution.py:99
  116.1 10.7 %fusion.5 = (f32[1576,768]{1,0:T(8,128)S(1)}, f32[1576,768]{1,0:T(8,128)S(1)}) fusion(bf16[2,384,768]{2,1,0:T(8,128)(2,1)S(1)} %copy-done.32, f32[1576,384]{1,0:T(8,128)S(1)} %get-tuple-element.77, f32[1576]{0:T(1024)S(1)} %add_rsqrt_fusion, f32[1576]{0:T(1024)S(1)} %broadcast_multiply_fusion.4, f32[384]{0:T(512)S(1)} %copy-done.47, ...), kind=kOutput, calls=%fused_computation.14 | convolution fusion | flops 1007631360 | bytes 12713984 | tf_op jit(solution)/shard_map/dot_general | solution.py:24
  126.9 3.7 add_convert_fusion
  132.1 2.9 fusion.67
  148.8 5.6 fusion.29
  158.1 3.6 multiply_reduce_fusion.1
  167.3 3.8 fusion.32
  171.8 4.6 multiply_reduce_fusion
  179.0 4.7 multiply_convert_fusion
  186.0 2.6 reshape.176
  191.7 2.5 copy.67
  194.2 2.6 reshape.177
  201.8 18.1 %all-gather.3.cloned.1.call-done = bf16[2048,384]{1,0:T(8,128)(2,1)} async-done(((bf16[128,384]{1,0:T(8,128)(2,1)}), bf16[2048,384]{1,0:T(8,128)(2,1)}) %all-gather.3.cloned.1.call-update) | async-done | bytes 1572880 | tf_op jit(solution)/shard_map/all_gather | solution.py:61
  223.7 2.7 fusion.130
  235.8 144.3 %all-reduce.16.cloned.1.call-done = (f32[4,384,192]{1,2,0:T(8,128)}, f32[2,384,768]{2,1,0:T(8,128)}) async-done(((f32[4,384,192]{1,2,0:T(8,128)}, f32[2,384,768]{2,1,0:T(8,128)}), (f32[4,384,192]{1,2,0:T(8,128)}, f32[2,384,768]{2,1,0:T(8,128)})) %all-reduce.16.cloned.1.call-update) | async-done | bytes 3538960 | tf_op jit(solution)/shard_map/psum | solution.py:430
  380.1 78.0 %rotated_update_768.1 = (f32[2,384,768]{2,1,0:T(8,128)}, bf16[2,384,768]{2,1,0:T(8,128)(2,1)}, f32[2,384,768]{2,1,0:T(8,128)}, f32[2,384,768]{2,1,0:T(8,128)}, f...) custom-call(f32[2,384,768]{2,1,0:T(8,128)} %get-tuple-element.94.grad_ref, f32[2,384,768]{2,1,0:T(8,128)} %weight_ref.1, ...), custom_call_target="tpu_custom_call" | custom-call | tf_op jit(solution)/shard_map/rotated_update_768/pallas_call | solution.py:306
  458.1 41.2 %rotated_update_384.1 = (f32[4,192,384]{2,1,0:T(8,128)}, bf16[4,192,384]{2,1,0:T(8,128)(2,1)}, f32[4,192,384]{2,1,0:T(8,128)}, f32[4,192,384]{2,1,0:T(8,128)}, f...) custom-call(f32[4,192,384]{2,1,0:T(8,128)} %bitcast.154, f32[4,192,384]{2,1,0:T(8,128)} %bitcast.153, ...), custom_call_target="tpu_custom_call" | custom-call | tf_op jit(solution)/shard_map/rotated_update_384/pallas_call | solution.py:306
  502.6 15.5 %convolution_convert_fusion = bf16[1576,384]{1,0:T(8,128)(2,1)} fusion(f32[384]{0:T(512)S(1)} %copy-done.48, f32[384]{0:T(512)S(1)} %copy-done.44, f32[1576]{0:T(1024)S(1)} %add_rsqrt_fusion.2, f32[1576]{0:T(1024)S(1)} %broadcast_multiply_fusion.6, bf16[2,384,768]{2,1,0:T(8,128)(2,1)} %convert_element_type.147, f32[1576,384]{1,0:T(8,128)} %get-tuple-element.70, ...), kind=kOutput, calls=%fused_computation.49 | convolution fusion | flops 1942640640 | bytes 6036800 | tf_op jit(solution)/shard_map/dot_general | solution.py:28
  518.2 2.9 multiply_reduce_fusion.2
  521.2 40.2 %all-reduce.1 = (f32[2,384]{1,0:T(2,128)S(1)}, f32[2,384]{1,0:T(2,128)S(1)}) all-reduce(f32[2,384]{1,0:T(2,128)S(1)} %pad_maximum_fusion.10, f32[2,384]{1,0:T(2,128)S(1)} %pad_maximum_fusion.9), channel_id=1, replica_groups=mesh['dp'=16,'mp'=2] {'dp'}, use_global_device_ids=true, to_apply=%region_27.28 | all-reduce | flops 1536 | bytes 12288 | tf_op jit(solution)/shard_map/psum | solution.py:430
  562.1 4.0 multiply_add_fusion
  566.1 3.9 add_convert_fusion.3
  (238 shorter events, 90.2 us)
Async XLA Ops:
  7.2 66.4 %all-gather.5.cloned.1.call-start = ((), (), s32[]{:S(2)}) async-start(), calls=%async_computation.2 | async-start | bytes 1671168 | tf_op jit(solution)/shard_map/all_gather | solution.py:61
  12.8 99.1 %copy-start = (f32[1576,384]{1,0:T(8,128)}, f32[1576,384]{1,0:T(8,128)S(1)}, u32[]{:S(2)}) copy-start(f32[1576,384]{1,0:T(8,128)S(1)} %convert_element_type.133) | copy-start | bytes 7262212
  12.9 99.0 %all-reduce.12.cloned.1.call-start = ((), (), s32[]{:S(2)}) async-start(), calls=%async_computation.3 | async-start | bytes 4841472 | tf_op jit(solution)/shard_map/psum | solution.py:99
  14.2 147.5 %copy-start.43 = (f32[384]{0:T(512)}, f32[384]{0:T(512)S(1)}, u32[]{:S(2)}) copy-start(f32[384]{0:T(512)S(1)} %get-tuple-element.63) | copy-start | bytes 4612
  14.2 4.2 copy-start.6
  34.1 8.1 %copy-start.57 = (s32[8,8]{1,0:T(8,128)S(1)}, s32[8,8]{1,0:T(8,128)}, u32[]{:S(2)}) copy-start(s32[8,8]{1,0:T(8,128)} %param.22) | copy-start | bytes 772
  91.3 66.8 %all-reduce.14.cloned.1.call-start = ((), (), s32[]{:S(2)}) async-start(), calls=%async_computation.4 | async-start | bytes 4841472 | tf_op jit(solution)/shard_map/psum | solution.py:381
  113.9 12.9 %copy-start.2 = (f32[1576,384]{1,0:T(8,128)}, f32[1576,384]{1,0:T(8,128)S(1)}, u32[]{:S(2)}) copy-start(f32[1576,384]{1,0:T(8,128)S(1)} %get-tuple-element.77) | copy-start | bytes 7262212
  116.1 10.8 %copy-start.25 = (bf16[1576,384]{1,0:T(8,128)(2,1)S(1)}, bf16[1576,384]{1,0:T(8,128)(2,1)}, u32[]{:S(2)}) copy-start(bf16[1576,384]{1,0:T(8,128)(2,1)} %param.19) | copy-start | bytes 3631108
  135.0 84.9 %all-gather.3.cloned.1.call-start = ((), (), s32[]{:S(2)}) async-start(), calls=%async_computation | async-start | bytes 1671168 | tf_op jit(solution)/shard_map/all_gather | solution.py:61
  135.6 244.6 %all-reduce.16.cloned.1.call-start = ((), (), s32[]{:S(2)}) async-start(), calls=%async_computation.5 | async-start | bytes 7077888 | tf_op jit(solution)/shard_map/psum | solution.py:430
  148.8 5.7 copy-start.3
  148.8 6.1 %copy-start.31 = (bf16[1576,768]{1,0:T(8,128)(2,1)S(1)}, bf16[1576,768]{1,0:T(8,128)(2,1)}, u32[]{:S(2)}) copy-start(bf16[1576,768]{1,0:T(8,128)(2,1)} %copy-done.30) | copy-start | bytes 7262212
  164.5 6.5 %slice-start = ((s8[4915200]{0:T(1024)(128)(4,1)}), s8[720896]{0:T(1024)(128)(4,1)S(1)}, s32[]{:S(2)}) async-start(s8[4915200]{0:T(1024)(128)(4,1)} %bitcast.150), calls=%async_computation.7 | async-start | bytes 1441792
  167.3 4.4 copy-start.36
  167.3 4.5 copy-start.38
  179.0 4.7 copy-start.14
  191.2 5.6 copy-start.5
  191.2 5.6 copy-start.16
  200.6 19.3 %copy-start.58 = (s32[64]{0:T(128)S(1)}, s32[64]{0:T(128)}, u32[]{:S(2)}) copy-start(s32[64]{0:T(128)} %eq.30) | copy-start | bytes 772
  201.7 21.0 %copy-start.28 = (bf16[8,197,3,64]{1,3,2,0:T(8,128)(2,1)S(1)}, bf16[8,197,3,64]{1,3,2,0:T(8,128)(2,1)}, u32[]{:S(2)}) copy-start(bf16[8,197,3,64]{1,3,2,0:T(8,128)(2,1)} %copy.54) | copy-start | bytes 1815556
  201.8 21.0 %copy-start.29 = (bf16[8,197,3,64]{1,0,3,2:T(8,128)(2,1)S(1)}, bf16[8,197,3,64]{1,0,3,2:T(8,128)(2,1)}, u32[]{:S(2)}) copy-start(bf16[8,197,3,64]{1,0,3,2:T(8,128)(2,1)} %reshape.167) | copy-start | bytes 1815556
  201.8 297.6 %all-reduce.18.cloned.1.call-start = ((), (), s32[]{:S(2)}) async-start(), calls=%async_computation.6 | async-start | bytes 9682944 | tf_op jit(solution)/shard_map/psum | solution.py:99
  235.2 330.9 %all-reduce.10.cloned.1.call-start = ((), (), s32[]{:S(2)}) async-start(), calls=%async_computation.1 | async-start | bytes 2420736 | tf_op jit(solution)/shard_map/psum | solution.py:105
  458.1 41.3 %copy-start.7 = (bf16[1576,384]{1,0:T(8,128)(2,1)S(1)}, bf16[1576,384]{1,0:T(8,128)(2,1)}, u32[]{:S(2)}) copy-start(bf16[1576,384]{1,0:T(8,128)(2,1)} %param.18) | copy-start | bytes 3631108
  502.6 15.6 %copy-start.1 = (f32[1576,384]{1,0:T(8,128)S(1)}, f32[1576,384]{1,0:T(8,128)}, u32[]{:S(2)}) copy-start(f32[1576,384]{1,0:T(8,128)} %copy-done) | copy-start | bytes 7262212
  502.6 15.6 %copy-start.40 = (f32[1576]{0:T(1024)S(1)}, f32[1576]{0:T(1024)}, u32[]{:S(2)}) copy-start(f32[1576]{0:T(1024)} %copy-done.39) | copy-start | bytes 18916
  502.6 15.6 %copy-start.42 = (f32[1576]{0:T(1024)S(1)}, f32[1576]{0:T(1024)}, u32[]{:S(2)}) copy-start(f32[1576]{0:T(1024)} %copy-done.41) | copy-start | bytes 18916
  502.6 15.6 %copy-start.46 = (f32[384]{0:T(512)S(1)}, f32[384]{0:T(512)}, u32[]{:S(2)}) copy-start(f32[384]{0:T(512)} %copy-done.45) | copy-start | bytes 4612
  518.2 43.2 %copy-start.50 = (f32[4,384]{1,0:T(4,128)S(1)}, f32[4,384]{1,0:T(4,128)}, u32[]{:S(2)}) copy-start(f32[4,384]{1,0:T(4,128)} %param.23) | copy-start | bytes 18436
  518.2 43.2 %copy-start.55 = (f32[4,384]{1,0:T(4,128)S(1)}, f32[4,384]{1,0:T(4,128)}, u32[]{:S(2)}) copy-start(f32[4,384]{1,0:T(4,128)} %param.25) | copy-start | bytes 18436
  518.2 43.2 %copy-start.56 = (f32[4,384]{1,0:T(4,128)S(1)}, f32[4,384]{1,0:T(4,128)}, u32[]{:S(2)}) copy-start(f32[4,384]{1,0:T(4,128)} %param.24) | copy-start | bytes 18436
  (38 other events, 86.4 us)
Sparse Core Ops, SparseCore 0:
  13.0 60.5 all-gather.4
  91.4 20.4 all-reduce.11
  135.1 22.9 all-reduce.13
  160.7 59.1 all-gather.2
  226.2 153.8 all-reduce.15
  383.3 28.4 all-reduce.17
  518.3 18.8 all-reduce.9
